TPU v7x, 32 devices: a whole 2x2x4 slice. The times are simulated.
32 devices in a mesh: wide: 8 (over y, x, core), narrow: 4 (over z).
Axes of the slice: x: 2, y: 2, z: 4, core: 2. Of those that a mesh axis runs over, the one named last changes fastest.
Arguments:
- coefficients: float32 [7, 7, 7, 32768], P(None, None, None, ('wide', 'narrow')), may hold values from -0.9 to 0.9
- degree: int32 [32768], P(('wide', 'narrow')), may hold values from 2 to 6
- new_degree: int32 [32768], P(('wide', 'narrow')), may hold values from 2 to 6
- face_link: int32 [6, 32768], P(None, ('wide', 'narrow')), may hold values from -1 to 1151, as said below
- send_index: int32 [4, 4096], P(None, ('wide', 'narrow')), may hold values from 0 to 1023, as said below
- new_owner: int32 [32768, 1], P(('wide', 'narrow')), may hold values from 0 to 31; in each aligned block of 1024 rows (0 to 1023, 1024 to 2047, ...) at most 64 rows name the same one
Outputs:
- moved: float32 [7, 7, 7, 65536], P(None, None, None, ('wide', 'narrow'))
Inputs may be any that keep to these rules, and one draw needn't show every extreme that they name: `face_link`: faces are numbered 0, 1 (lower, upper x), 2, 3 (y), 4, 5 (z). Each device holds a box of 8 x 16 x 8 elements of a grid; the box across its x sides belongs to the device with the previous or next index of wide and the same narrow index, across its z sides to the device with the previous or next index of narrow and the same wide index. A value below 1024 names the neighbour among the same device's elements; a value 1024 + t names slot t of the neighbouring device's row of send_index (row 1, 0, 3, 2 for faces 0, 1, 4, 5); -1 marks the grid's outer boundary. The neighbour across face f sees the element across its face f xor 1. `send_index`: row 0, 1, 2, 3 lists the device's elements on the lower x, upper x, lower z, upper z side of its box, each once, in the slot order that face_link uses. `new_owner`: the elements of one device name any one device (itself included) at most 64 times, and some device is named exactly 64 times.
All inputs are finite; a program needn't handle non-finite values.
Results may differ from a plain program's by a relative error of at most 0.0003.
Values sent between devices are 32-bit elements; how exact they have to be, the bound alone decides.
A program may use at most 192 MiB of HBM per device.

v0:
```python
import functools

import jax
import jax.numpy as jnp
import numpy as np
from jax import lax
from jax.experimental import pallas as pl
from jax.experimental.pallas import tpu as pltpu
from jax.sharding import PartitionSpec as P

MODES = 7
QUAD = 8
SIDE = 8
DEPTH = 16
LANES = 128
ROWS = 352
FACE = 56
PAIR = 2 * FACE
TRACE = 6 * PAIR
WORK = 256
STEP_SIZE = 0.0003
MESH = pl.DeviceIdType.MESH
F32 = jnp.float32
BF16 = jnp.bfloat16


def legendre_rows(points, count):
    values = [points * 0.0 + 1.0, points.copy()]
    slopes = [points * 0.0, points * 0.0 + 1.0]
    for order in range(1, count):
        values.append(
            ((2.0 * order + 1.0) * points * values[order] - order * values[order - 1])
            / (order + 1.0)
        )
        slopes.append(slopes[order - 1] + (2.0 * order + 1.0) * values[order])
    return (np.stack(values[: count + 1]), np.stack(slopes[: count + 1]))


def gauss_rule(count):
    points = np.cos(np.pi * (np.arange(count) + 0.75) / (count + 0.5))
    for sweep in range(60):
        values, slopes = legendre_rows(points, count)
        points = points - values[count] / slopes[count]
    values, slopes = legendre_rows(points, count)
    weights = 2.0 / ((1.0 - points * points) * slopes[count] ** 2)
    return (points[::-1], weights[::-1])


def operators():
    points, weights = gauss_rule(QUAD)
    scales = np.sqrt((2.0 * np.arange(MODES) + 1.0) / 2.0)
    value_rows, slope_rows = legendre_rows(points, MODES)
    values = value_rows[:MODES].T * scales
    slopes = slope_rows[:MODES].T * scales
    stiffness = slopes.T @ (weights[:, None] * slopes)
    project = (values * weights[:, None]).T
    orders = np.arange(MODES)
    ends = np.stack([(-1.0) ** orders, np.ones(MODES)]) * scales
    end_slopes = (
        np.stack([(-1.0) ** (orders + 1), np.ones(MODES)]) * (orders * (orders + 1) / 2.0) * scales
    )
    eye = np.eye(MODES)

    def kron(first, second, third):
        return np.kron(first, np.kron(second, third))

    modes = MODES**3
    evaluate = np.zeros((QUAD**3, ROWS))
    evaluate[:, :modes] = kron(values, values, values)
    back = np.zeros((ROWS, QUAD**3))
    back[:modes] = kron(project, project, project)
    trace = np.zeros((TRACE, ROWS))
    plane = MODES**2
    for face in range(6):
        axis, side = divmod(face, 2)
        for kind, vector in enumerate((ends[side], end_slopes[side])):
            parts = [eye, eye, eye]
            parts[axis] = vector[None, :]
            base = face * PAIR + kind * FACE
            trace[base : base + plane, :modes] = kron(*parts)
    inner = kron(stiffness, eye, eye) + kron(eye, stiffness, eye) + kron(eye, eye, stiffness)
    gather = np.zeros((ROWS, TRACE + ROWS))
    gather[:, :TRACE] = trace.T
    gather[:modes, TRACE : TRACE + modes] = -inner
    return evaluate, back, trace, gather


def host_halves(array):
    high = array.astype(jnp.bfloat16)
    low = (array - high.astype(np.float64)).astype(jnp.bfloat16)
    return jnp.stack([jnp.asarray(high), jnp.asarray(low)])


def highest_modes():
    order = np.arange(MODES)
    top = np.maximum(np.maximum(order[:, None, None], order[None, :, None]), order[None, None, :])
    column = np.full((ROWS, LANES), 99, np.int32)
    column[: MODES**3] = top.reshape(-1)[:, None]
    return jnp.asarray(column)


def split(array):
    high = array.astype(BF16)
    return high, (array - high.astype(F32)).astype(BF16)


def product(table_ref, high, low):
    def dot(left, right):
        return jnp.dot(left, right, preferred_element_type=F32)

    return dot(table_ref[0], high) + (dot(table_ref[0], low) + dot(table_ref[1], high))


def take(table, index):
    row, lane = index >> 7, index & (LANES - 1)
    result = jnp.zeros_like(table)
    for s in range(table.shape[0]):
        line = jnp.broadcast_to(table[s : s + 1, :], table.shape)
        result = jnp.where(row == s, jnp.take_along_axis(line, lane, axis=1), result)
    return result


def arrange(
    devices, capacity, coef_ref, degree_ref, new_degree_ref, link_ref, owner_ref, top_ref,
    start_ref, aux_ref, flat_ref, pair_ref,
):
    rows = SIDE
    count = rows * LANES
    iota = lax.broadcasted_iota
    sub, lane = iota(jnp.int32, (rows, LANES), 0), iota(jnp.int32, (rows, LANES), 1)
    own = sub * LANES + lane
    links = [
        jnp.concatenate(
            [link_ref[face : face + 1, b * LANES : (b + 1) * LANES] for b in range(rows)], axis=0
        )
        for face in range(6)
    ]
    inside = [(link >= 0) & (link < count) for link in links]
    corner = ~(inside[0] | inside[2] | inside[4])
    first = jnp.sum(jnp.where(corner, own, 0).astype(F32), axis=1, keepdims=True)
    first = jnp.sum(first, axis=0, keepdims=True).astype(jnp.int32)
    order = jnp.broadcast_to(first, (rows, LANES))
    for face, place, bits in ((3, lane & (DEPTH - 1), 4), (5, lane >> 4, 3), (1, sub, 3)):
        step = jnp.where(inside[face], links[face], own)
        for bit in range(bits):
            order = jnp.where(((place >> bit) & 1) == 1, take(step, order), order)
            if bit < bits - 1:
                step = take(step, step)
    owner = owner_ref[...]
    before = (iota(jnp.int32, (LANES, LANES), 0) < iota(jnp.int32, (LANES, LANES), 1)).astype(F32)
    before = before.astype(BF16)
    base = jnp.zeros((devices, 1), F32)
    lines = []
    for b in range(rows):
        named = (iota(jnp.int32, (devices, LANES), 0) == owner[b : b + 1, :]).astype(F32)
        earlier = jnp.dot(named.astype(BF16), before, preferred_element_type=F32) + base
        lines.append(jnp.sum(named * earlier, axis=0, keepdims=True))
        base = base + jnp.sum(named, axis=1, keepdims=True)
    rank = jnp.concatenate(lines, axis=0).astype(jnp.int32)
    column = take(owner * capacity + rank, order)
    degree = take(degree_ref[...], order)
    new_degree = take(new_degree_ref[...], order)
    aux_ref[...] = jnp.zeros_like(aux_ref)
    for b in range(rows):
        at = slice(b * LANES, (b + 1) * LANES)
        for row, array in enumerate((degree, new_degree, column, order)):
            aux_ref[row : row + 1, at] = array[b : b + 1, :]
    flat_ref[ROWS - 16 :, :] = jnp.zeros((16, count), F32)
    for i in range(MODES):
        for j in range(MODES):
            at = (i * MODES + j) * MODES
            flat_ref[at : at + MODES, :] = coef_ref[i, j]
    high, low = split(flat_ref[...])
    pair_ref[:ROWS, :] = high
    pair_ref[ROWS:, :] = low
    top = top_ref[:, :1]

    def body(c, carry):
        at = pl.ds(pl.multiple_of(c * WORK, WORK), WORK)
        chooser = (iota(jnp.int32, (count, WORK), 0) == aux_ref[3:4, at]).astype(F32).astype(BF16)
        both = jnp.dot(pair_ref[...], chooser, preferred_element_type=F32)
        mask = top <= aux_ref[0:1, at]
        start_ref[:, at] = jnp.where(mask, both[:ROWS] + both[ROWS:], 0.0)
        return carry

    lax.fori_loop(0, count // WORK, body, 0)


def evolve(
    wide, narrow, capacity, start_ref, aux_ref, top_ref, eval_ref, back_ref, trace_ref, gather_ref,
    out_ref,
    state_ref, face_refs, up_ref, down_ref, high_ref, low_ref, pair_ref, send_ref,
    z_out, z_in, halo_send, halo_recv, send_sem, recv_sem, local_sem,
):
    devices = wide * narrow
    count = start_ref.shape[1]
    w, n = lax.axis_index("wide"), lax.axis_index("narrow")
    me = w * narrow + n
    barrier = pltpu.get_barrier_semaphore()

    def greet(k, carry):
        other = lax.rem(me + k, devices)
        pl.semaphore_signal(
            barrier, inc=1, device_id=(other // narrow, lax.rem(other, narrow)), device_id_type=MESH
        )
        return carry

    lax.fori_loop(1, devices, greet, 0)
    top = top_ref[:, :1]
    iota = lax.broadcasted_iota
    lane = iota(jnp.int32, (PAIR, LANES), 1)
    flip = jnp.where(iota(jnp.int32, (PAIR, LANES), 0) < FACE, -1.0, 1.0)

    def local_part(source_ref):
        def body(c, carry):
            at = pl.ds(pl.multiple_of(c * WORK, WORK), WORK)
            values = product(eval_ref, *split(source_ref[:, at]))
            values = values + values * values * values * (1.0 / 3.0)
            field = jnp.where(top <= aux_ref[0:1, at], product(back_ref, *split(values)), 0.0)
            high, low = split(field)
            high_ref[TRACE:, at] = high
            low_ref[TRACE:, at] = low
            traces = product(trace_ref, high, low)
            down_ref[:, at] = traces[:PAIR]
            up_ref[:, pl.ds(pl.multiple_of(c * WORK + LANES, LANES), WORK)] = traces[
                PAIR : 2 * PAIR
            ]
            for face in range(2, 6):
                face_refs[face - 2, :, at] = traces[face * PAIR : (face + 1) * PAIR]
            return carry

        lax.fori_loop(0, count // WORK, body, 0)

    def exchange(turn):
        low_side = jnp.zeros((PAIR, LANES), F32)
        high_side = jnp.zeros((PAIR, LANES), F32)
        for b in range(SIDE):
            at = slice(b * LANES, (b + 1) * LANES)
            mine = (lane >> 4) == b
            lower = face_refs[2, :, at]
            upper = face_refs[3, :, at]
            shift = b * DEPTH
            low_side = jnp.where(mine, pltpu.roll(lower, shift, 1) if shift else lower, low_side)
            shift = (b * DEPTH + DEPTH) % LANES
            high_side = jnp.where(mine, pltpu.roll(upper, shift, 1) if shift else upper, high_side)
        z_out[turn, 0] = low_side
        z_out[turn, 1] = high_side
        plans = (
            (w > 0, z_out.at[turn, 2], z_in.at[turn, 3], (w - 1, n)),
            (w < wide - 1, z_out.at[turn, 3], z_in.at[turn, 2], (w + 1, n)),
            (n > 0, z_out.at[turn, 0], z_in.at[turn, 1], (w, n - 1)),
            (n < narrow - 1, z_out.at[turn, 1], z_in.at[turn, 0], (w, n + 1)),
        )
        z_out[turn, 2] = down_ref[:, 0:LANES]
        z_out[turn, 3] = up_ref[:, count : count + LANES]
        into = (3, 2, 1, 0)
        side_of = (2, 3, 0, 1)

        def copy(k):
            return pltpu.make_async_remote_copy(
                src_ref=plans[k][1],
                dst_ref=plans[k][2],
                send_sem=halo_send.at[turn, k],
                recv_sem=halo_recv.at[turn, into[k]],
                device_id=plans[k][3],
                device_id_type=MESH,
            )

        for k in range(4):
            pl.when(plans[k][0])(lambda k=k: copy(k).start())

        def finish():
            for k in range(4):
                slot = side_of[k]

                def arrive(k=k, slot=slot):
                    pltpu.make_async_remote_copy(
                        src_ref=plans[k][1],
                        dst_ref=z_in.at[turn, slot],
                        send_sem=halo_send.at[turn, k],
                        recv_sem=halo_recv.at[turn, slot],
                        device_id=plans[k][3],
                        device_id_type=MESH,
                    ).wait()

                def mirror(slot=slot):
                    z_in[turn, slot] = z_out[turn, slot] * flip

                pl.when(plans[k][0])(arrive)
                pl.when(jnp.logical_not(plans[k][0]))(mirror)
            up_ref[:, 0:LANES] = z_in[turn, 2]
            down_ref[:, count : count + LANES] = z_in[turn, 3]

        return finish

    def terms(turn, b, faces):
        at = slice(b * LANES, (b + 1) * LANES)
        later = slice((b + 1) * LANES, (b + 2) * LANES)
        sigma = (aux_ref[0:1, at] + 1).astype(F32)
        sigma = sigma * sigma
        for face in faces:
            sign = 2.0 * (face % 2) - 1.0
            if face == 0:
                own, ghost = down_ref[:, at], up_ref[:, at]
            elif face == 1:
                own, ghost = up_ref[:, later], down_ref[:, later]
            else:
                own, other = face_refs[face - 2, :, at], face_refs[(face ^ 1) - 2, :, at]
                if face == 2:
                    edge, ghost = (lane & (DEPTH - 1)) == 0, pltpu.roll(other, 1, 1)
                    outer = own * flip
                elif face == 3:
                    edge, ghost = (lane & (DEPTH - 1)) == DEPTH - 1, pltpu.roll(other, LANES - 1, 1)
                    outer = own * flip
                elif face == 4:
                    edge, ghost = (lane >> 4) == 0, pltpu.roll(other, DEPTH, 1)
                    shift = (LANES - b * DEPTH) % LANES
                    outer = z_in[turn, 0]
                    outer = pltpu.roll(outer, shift, 1) if shift else outer
                else:
                    edge, ghost = (lane >> 4) == SIDE - 1, pltpu.roll(other, LANES - DEPTH, 1)
                    shift = (LANES - DEPTH - b * DEPTH) % LANES
                    outer = z_in[turn, 1]
                    outer = pltpu.roll(outer, shift, 1) if shift else outer
                ghost = jnp.where(edge, outer, ghost)
            jump = own[:FACE] - ghost[:FACE]
            sums = own[FACE:] + ghost[FACE:]
            base = face * PAIR
            both = jnp.concatenate(
                [(0.5 * sign) * sums - sigma * jump, (0.5 * sign) * jump], axis=0
            )
            high, low = split(both)
            high_ref[base : base + PAIR, at] = high
            low_ref[base : base + PAIR, at] = low

    def residual(c):
        at = pl.ds(pl.multiple_of(c * WORK, WORK), WORK)
        rate = product(gather_ref, high_ref[:, at], low_ref[:, at])
        return at, jnp.where(top <= aux_ref[0:1, at], rate, 0.0) * STEP_SIZE

    def section(turn, source_ref, before_send, store):
        local_part(source_ref)
        before_send()
        finish = exchange(turn)
        for b in range(SIDE):
            terms(turn, b, (2, 3))
        finish()
        for b in range(SIDE):
            terms(turn, b, (0, 1, 4, 5))
        lax.fori_loop(0, count // WORK, store, 0)

    def store_first(c, carry):
        at, change = residual(c)
        state_ref[:, at] = start_ref[:, at] + change
        return carry

    def store_second(c, carry):
        at, change = residual(c)
        second = 0.5 * (start_ref[:, at] + state_ref[:, at] + change)
        high, low = split(jnp.where(top <= aux_ref[1:2, at], second, 0.0))
        pair_ref[:ROWS, at] = high
        pair_ref[ROWS:, at] = low
        return carry

    section(0, start_ref, lambda: pl.semaphore_wait(barrier, devices - 1), store_first)
    section(1, state_ref, lambda: None, store_second)

    share = LANES // capacity
    height = send_ref.shape[1]
    tiles = devices * capacity // LANES
    first_tile = me // share
    wide_lane = iota(jnp.int32, (height, LANES), 1)

    def outgoing(other):
        return pltpu.make_async_remote_copy(
            src_ref=send_ref.at[other],
            dst_ref=out_ref.at[me],
            send_sem=send_sem.at[other],
            recv_sem=recv_sem.at[me],
            device_id=(other // narrow, lax.rem(other, narrow)),
            device_id_type=MESH,
        )

    def place(t, carry):
        tile = lax.rem(first_tile + t, tiles)
        slot = iota(jnp.int32, (LANES, count), 0) + tile * LANES
        chooser = (slot == aux_ref[2:3, :]).astype(F32).astype(BF16)
        both = lax.dot_general(
            pair_ref[...], chooser, (((1,), (1,)), ((), ())), preferred_element_type=F32
        )
        columns = both[:ROWS] + both[ROWS:]
        if share * height > ROWS:
            columns = jnp.concatenate(
                [columns, jnp.zeros((share * height - ROWS, LANES), F32)], axis=0
            )
        for j in range(share):
            block = jnp.zeros((height, LANES), F32)
            for q in range(share):
                piece = columns[q * height : (q + 1) * height]
                shift = ((q - j) * capacity) % LANES
                piece = pltpu.roll(piece, shift, 1) if shift else piece
                block = jnp.where(wide_lane // capacity == q, piece, block)
            other = tile * share + j
            send_ref[other] = block

            @pl.when(other != me)
            def _():
                outgoing(other).start()

        return carry

    lax.fori_loop(0, tiles, place, 0)
    own = pltpu.make_async_copy(send_ref.at[me], out_ref.at[me], local_sem)
    own.start()

    def collect(k, carry):
        source = lax.rem(me + devices - k, devices)
        pltpu.make_async_remote_copy(
            src_ref=send_ref.at[source],
            dst_ref=out_ref.at[source],
            send_sem=send_sem.at[source],
            recv_sem=recv_sem.at[source],
            device_id=(source // narrow, lax.rem(source, narrow)),
            device_id_type=MESH,
        ).wait()
        return carry

    lax.fori_loop(1, devices, collect, 0)
    own.wait()


def unpack(capacity, block_ref, moved_ref, flat_ref):
    share, height, _ = block_ref.shape
    lane = lax.broadcasted_iota(jnp.int32, (height, LANES), 1)
    for q in range(share):
        piece = jnp.zeros((height, LANES), F32)
        for j in range(share):
            shift = ((j - q) * capacity) % LANES
            block = block_ref[j]
            block = pltpu.roll(block, shift, 1) if shift else block
            piece = jnp.where(lane // capacity == j, block, piece)
        flat_ref[q * height : (q + 1) * height, :] = piece
    for i in range(MODES):
        for j in range(MODES):
            at = (i * MODES + j) * MODES
            moved_ref[i, j] = flat_ref[at : at + MODES, :]


def on_device(coefficients, degree, new_degree, face_link, send_index, new_owner):
    wide, narrow = lax.axis_size("wide"), lax.axis_size("narrow")
    devices = wide * narrow
    count = coefficients.shape[3]
    capacity = max(2, 2 * count // devices)
    share = LANES // capacity
    modes = MODES**3
    height = -(-(-(-modes // share)) // 8) * 8
    evaluate, back, trace, gather = (host_halves(array) for array in operators())
    top = highest_modes()
    vmem = pl.BlockSpec(memory_space=pltpu.VMEM)
    square = (SIDE, LANES)
    start, aux = pl.pallas_call(
        functools.partial(arrange, devices, capacity),
        out_shape=(
            jax.ShapeDtypeStruct((ROWS, count), F32),
            jax.ShapeDtypeStruct((8, count), jnp.int32),
        ),
        in_specs=[vmem] * 6,
        out_specs=(vmem, vmem),
        scratch_shapes=[pltpu.VMEM((ROWS, count), F32), pltpu.VMEM((2 * ROWS, count), BF16)],
        compiler_params=pltpu.CompilerParams(vmem_limit_bytes=48 * 2**20),
        name="arrange",
    )(
        coefficients,
        degree.reshape(square),
        new_degree.reshape(square),
        face_link,
        new_owner.reshape(square),
        top,
    )
    blocks = pl.pallas_call(
        functools.partial(evolve, wide, narrow, capacity),
        out_shape=jax.ShapeDtypeStruct((devices, height, LANES), F32),
        in_specs=[vmem] * 7,
        out_specs=pl.BlockSpec(memory_space=pl.ANY),
        scratch_shapes=[
            pltpu.VMEM((ROWS, count), F32),
            pltpu.VMEM((4, PAIR, count), F32),
            pltpu.VMEM((PAIR, count + LANES), F32),
            pltpu.VMEM((PAIR, count + LANES), F32),
            pltpu.VMEM((TRACE + ROWS, count), BF16),
            pltpu.VMEM((TRACE + ROWS, count), BF16),
            pltpu.VMEM((2 * ROWS, count), BF16),
            pltpu.VMEM((devices, height, LANES), F32),
            pltpu.VMEM((2, 4, PAIR, LANES), F32),
            pltpu.VMEM((2, 4, PAIR, LANES), F32),
            pltpu.SemaphoreType.DMA((2, 4)),
            pltpu.SemaphoreType.DMA((2, 4)),
            pltpu.SemaphoreType.DMA((devices,)),
            pltpu.SemaphoreType.DMA((devices,)),
            pltpu.SemaphoreType.DMA,
        ],
        compiler_params=pltpu.CompilerParams(
            collective_id=0, has_side_effects=True, vmem_limit_bytes=56 * 2**20
        ),
        name="evolve",
    )(start, aux, top, evaluate, back, trace, gather)
    return pl.pallas_call(
        functools.partial(unpack, capacity),
        grid=(devices // share,),
        out_shape=jax.ShapeDtypeStruct((MODES, MODES, MODES, devices * capacity), F32),
        in_specs=[pl.BlockSpec((share, height, LANES), lambda t: (t, 0, 0))],
        out_specs=pl.BlockSpec((MODES, MODES, MODES, LANES), lambda t: (0, 0, 0, t)),
        scratch_shapes=[pltpu.VMEM((share * height, LANES), F32)],
        compiler_params=pltpu.CompilerParams(vmem_limit_bytes=32 * 2**20),
        name="unpack",
    )(blocks)


def solution(mesh):
    placed = (
        P(None, None, None, ("wide", "narrow")),
        P(("wide", "narrow")),
        P(("wide", "narrow")),
        P(None, ("wide", "narrow")),
        P(None, ("wide", "narrow")),
        P(("wide", "narrow"), None),
    )
    return jax.shard_map(
        on_device,
        mesh=mesh,
        in_specs=placed,
        out_specs=P(None, None, None, ("wide", "narrow")),
        check_vma=False,
    )
```

profile of v0, /device:TPU:0, one launch (start us, length us, event | category | flops | bytes accessed | tf_op | source)
XLA Modules:
  0.0 123.7 jit_solution(6809222663552065235)
XLA Ops:
  0.0 0.0 copy-start.1
  0.0 1.4 %copy-done.1 = f32[7,7,7,1024]{3,2,1,0:T(8,128)S(1)} copy-done((f32[7,7,7,1024]{3,2,1,0:T(8,128)S(1)}, f32[7,7,7,1024]{3,2,1,0:T(8,128)}, u32[]{:S(2)}) %copy-start.1) | copy-done | bytes 1404952
  1.4 0.0 copy-start.3
  1.4 0.9 copy-done.3
  2.3 0.0 copy-start.4
  2.3 0.8 copy-done.4
  3.1 0.0 copy-start.6
  3.1 0.7 copy-done.6
  3.8 0.0 copy-start.7
  3.8 0.7 copy-done.7
  4.5 0.0 copy-start.8
  4.5 0.7 copy-done.8
  5.2 3.8 %arrange.1 = (f32[352,1024]{1,0:T(8,128)S(1)}, s32[8,1024]{1,0:T(8,128)S(1)}) custom-call(f32[7,7,7,1024]{3,2,1,0:T(8,128)S(1)} %copy-done.1, s32[8,128]{1,0:T(8,128)S(1)} %bitcast.3, s32[8,128]{1,0:T(8,128)S(1)} %bitcast.4, s32[6,1024]{1,0:T(8,128)S(1)} %copy-done.4, s32[8,128]{1,0:T(8,128)S(1)} %bitcast.5, s32[352,128]{1,0:T(8,128)S(1)} %copy-done.3), custom_call_target="tpu_custom_call" | custom-call | tf_op jit(solution)/shard_map/arrange/pallas_call | solution.py:461
  9.0 0.0 copy-start.2
  9.0 1.1 copy-done.2
  10.1 0.0 copy-start.5
  10.1 0.6 copy-done.5
  10.7 104.5 %evolve.1.block_ref = f32[32,176,128]{2,1,0:T(8,128)} custom-call(f32[352,1024]{1,0:T(8,128)} %copy-done.2, s32[8,1024]{1,0:T(8,128)} %copy-done.5, s32[352,128]{1,0:T(8,128)} %constant.26.clone.top_ref, bf16[2,512,352]{2,1,0:T(8,128)(2,1)} %constant.29.eval_ref, bf16[2,352,512]{2,1,0:T(8,128)(2,1)} %constant.32.back_ref, ...), custom_call_target="tpu_custom_call" | custom-call | tf_op jit(solution)/shard_map/evolve/pallas_call | solution.py:480
  115.2 0.0 copy-start
  115.2 1.8 %copy-done = f32[32,176,128]{2,1,0:T(8,128)S(1)} copy-done((f32[32,176,128]{2,1,0:T(8,128)S(1)}, f32[32,176,128]{2,1,0:T(8,128)}, u32[]{:S(2)}) %copy-start) | copy-done | bytes 2883608
  117.0 6.7 %unpack.1 = f32[7,7,7,2048]{3,2,1,0:T(8,128)} custom-call(f32[32,176,128]{2,1,0:T(8,128)S(1)} %copy-done), custom_call_target="tpu_custom_call" | custom-call | tf_op jit(solution)/shard_map/unpack/pallas_call | solution.py:507
Async XLA Ops:
  0.0 1.4 %copy-start.1 = (f32[7,7,7,1024]{3,2,1,0:T(8,128)S(1)}, f32[7,7,7,1024]{3,2,1,0:T(8,128)}, u32[]{:S(2)}) copy-start(f32[7,7,7,1024]{3,2,1,0:T(8,128)} %coef_ref.1) | copy-start | bytes 4214788
  1.4 0.9 copy-start.3
  2.3 0.8 copy-start.4
  3.1 0.7 copy-start.6
  3.8 0.7 copy-start.7
  4.5 0.7 copy-start.8
  9.0 1.1 copy-start.2
  10.1 0.6 copy-start.5
  115.2 1.8 %copy-start = (f32[32,176,128]{2,1,0:T(8,128)S(1)}, f32[32,176,128]{2,1,0:T(8,128)}, u32[]{:S(2)}) copy-start(f32[32,176,128]{2,1,0:T(8,128)} %evolve.1.block_ref) | copy-start | bytes 8650756
where the time goes:
time: 124 us
  Pallas kernels  115 us (93%)
  local copies, waits for them, and re-layouts  8.67 us (7%)
    pallas_call x1, Pallas kernels, on_device(): pl.pallas_call(functools.partial(evolve, wide, narrow, capacity), out_sha...  105 us
    unnamed x18, local copies, waits for them, and re-layouts  8.67 us
    pallas_call x1, Pallas kernels, on_device(): pl.pallas_call(functools.partial(unpack, capacity), grid=(devices // shar...  6.67 us
    pallas_call x1, Pallas kernels, on_device(): pl.pallas_call(functools.partial(arrange, devices, capacity), out_shape=(...  3.8 us

commit v1 on v0

--- a/solution.py
+++ b/solution.py
@@ -187,16 +187,24 @@
 
 
 def evolve(
-    wide, narrow, capacity, start_ref, aux_ref, top_ref, eval_ref, back_ref, trace_ref, gather_ref,
-    out_ref,
-    state_ref, face_refs, up_ref, down_ref, high_ref, low_ref, pair_ref, send_ref,
-    z_out, z_in, halo_send, halo_recv, send_sem, recv_sem, local_sem,
+    wide, narrow, capacity, aux_ref, top_ref, start_at, eval_at, back_at, trace_at, gather_at,
+    moved_ref,
+    start_ref, eval_ref, back_ref, trace_ref, gather_ref, table_sem, recv_ref, flat_ref, state_ref, face_refs, up_ref, down_ref, high_ref, low_ref, pair_ref, send_ref,
+    z_out, z_in, halo_send, halo_recv, send_sem, recv_sem,
 ):
     devices = wide * narrow
     count = start_ref.shape[1]
     w, n = lax.axis_index("wide"), lax.axis_index("narrow")
     me = w * narrow + n
     barrier = pltpu.get_barrier_semaphore()
+    pairs = ((start_at, start_ref), (eval_at, eval_ref), (back_at, back_ref))
+    pairs = pairs + ((trace_at, trace_ref), (gather_at, gather_ref))
+    loads = [
+        pltpu.make_async_copy(source, target, table_sem.at[i])
+        for i, (source, target) in enumerate(pairs)
+    ]
+    for load in loads:
+        load.start()
 
     def greet(k, carry):
         other = lax.rem(me + k, devices)
@@ -349,6 +357,10 @@
             terms(turn, b, (0, 1, 4, 5))
         lax.fori_loop(0, count // WORK, store, 0)
 
+    def enter():
+        loads[4].wait()
+        pl.semaphore_wait(barrier, devices - 1)
+
     def store_first(c, carry):
         at, change = residual(c)
         state_ref[:, at] = start_ref[:, at] + change
@@ -362,19 +374,21 @@
         pair_ref[ROWS:, at] = low
         return carry
 
-    section(0, start_ref, lambda: pl.semaphore_wait(barrier, devices - 1), store_first)
+    for load in loads[:4]:
+        load.wait()
+    section(0, start_ref, enter, store_first)
     section(1, state_ref, lambda: None, store_second)
 
     share = LANES // capacity
     height = send_ref.shape[1]
     tiles = devices * capacity // LANES
-    first_tile = me // share
+    first_tile = me // share + 1
     wide_lane = iota(jnp.int32, (height, LANES), 1)
 
     def outgoing(other):
         return pltpu.make_async_remote_copy(
             src_ref=send_ref.at[other],
-            dst_ref=out_ref.at[me],
+            dst_ref=recv_ref.at[me],
             send_sem=send_sem.at[other],
             recv_sem=recv_sem.at[me],
             device_id=(other // narrow, lax.rem(other, narrow)),
@@ -401,49 +415,52 @@
                 piece = pltpu.roll(piece, shift, 1) if shift else piece
                 block = jnp.where(wide_lane // capacity == q, piece, block)
             other = tile * share + j
-            send_ref[other] = block
+
+            @pl.when(other == me)
+            def _(block=block):
+                recv_ref[me] = block
 
             @pl.when(other != me)
-            def _():
+            def _(block=block, other=other):
+                send_ref[other] = block
                 outgoing(other).start()
 
         return carry
 
     lax.fori_loop(0, tiles, place, 0)
-    own = pltpu.make_async_copy(send_ref.at[me], out_ref.at[me], local_sem)
-    own.start()
-
-    def collect(k, carry):
-        source = lax.rem(me + devices - k, devices)
-        pltpu.make_async_remote_copy(
-            src_ref=send_ref.at[source],
-            dst_ref=out_ref.at[source],
-            send_sem=send_sem.at[source],
-            recv_sem=recv_sem.at[source],
-            device_id=(source // narrow, lax.rem(source, narrow)),
-            device_id_type=MESH,
-        ).wait()
+
+    def collect(t, carry):
+        tile = lax.rem(first_tile + tiles - t, tiles)
+        pieces = [jnp.zeros((height, LANES), F32) for _ in range(share)]
+        for j in range(share):
+            source = tile * share + j
+
+            @pl.when(source != me)
+            def _(source=source):
+                pltpu.make_async_remote_copy(
+                    src_ref=send_ref.at[source],
+                    dst_ref=recv_ref.at[source],
+                    send_sem=send_sem.at[source],
+                    recv_sem=recv_sem.at[source],
+                    device_id=(source // narrow, lax.rem(source, narrow)),
+                    device_id_type=MESH,
+                ).wait()
+
+            block = recv_ref[source]
+            for q in range(share):
+                shift = ((j - q) * capacity) % LANES
+                moved = pltpu.roll(block, shift, 1) if shift else block
+                pieces[q] = jnp.where(wide_lane // capacity == j, moved, pieces[q])
+        for q in range(share):
+            flat_ref[q * height : (q + 1) * height, :] = pieces[q]
+        at = pl.ds(pl.multiple_of(tile * LANES, LANES), LANES)
+        for i in range(MODES):
+            for j in range(MODES):
+                row = (i * MODES + j) * MODES
+                moved_ref[i, j, :, at] = flat_ref[row : row + MODES, :]
         return carry
 
-    lax.fori_loop(1, devices, collect, 0)
-    own.wait()
-
-
-def unpack(capacity, block_ref, moved_ref, flat_ref):
-    share, height, _ = block_ref.shape
-    lane = lax.broadcasted_iota(jnp.int32, (height, LANES), 1)
-    for q in range(share):
-        piece = jnp.zeros((height, LANES), F32)
-        for j in range(share):
-            shift = ((j - q) * capacity) % LANES
-            block = block_ref[j]
-            block = pltpu.roll(block, shift, 1) if shift else block
-            piece = jnp.where(lane // capacity == j, block, piece)
-        flat_ref[q * height : (q + 1) * height, :] = piece
-    for i in range(MODES):
-        for j in range(MODES):
-            at = (i * MODES + j) * MODES
-            moved_ref[i, j] = flat_ref[at : at + MODES, :]
+    lax.fori_loop(0, tiles, collect, 0)
 
 
 def on_device(coefficients, degree, new_degree, face_link, send_index, new_owner):
@@ -477,12 +494,21 @@
         new_owner.reshape(square),
         top,
     )
-    blocks = pl.pallas_call(
+    anywhere = pl.BlockSpec(memory_space=pl.ANY)
+    return pl.pallas_call(
         functools.partial(evolve, wide, narrow, capacity),
-        out_shape=jax.ShapeDtypeStruct((devices, height, LANES), F32),
-        in_specs=[vmem] * 7,
-        out_specs=pl.BlockSpec(memory_space=pl.ANY),
+        out_shape=jax.ShapeDtypeStruct((MODES, MODES, MODES, devices * capacity), F32),
+        in_specs=[vmem] * 2 + [anywhere] * 5,
+        out_specs=vmem,
         scratch_shapes=[
+            pltpu.VMEM((ROWS, count), F32),
+            pltpu.VMEM(evaluate.shape, BF16),
+            pltpu.VMEM(back.shape, BF16),
+            pltpu.VMEM(trace.shape, BF16),
+            pltpu.VMEM(gather.shape, BF16),
+            pltpu.SemaphoreType.DMA((5,)),
+            pltpu.VMEM((devices, height, LANES), F32),
+            pltpu.VMEM((share * height, LANES), F32),
             pltpu.VMEM((ROWS, count), F32),
             pltpu.VMEM((4, PAIR, count), F32),
             pltpu.VMEM((PAIR, count + LANES), F32),
@@ -497,23 +523,12 @@
             pltpu.SemaphoreType.DMA((2, 4)),
             pltpu.SemaphoreType.DMA((devices,)),
             pltpu.SemaphoreType.DMA((devices,)),
-            pltpu.SemaphoreType.DMA,
         ],
         compiler_params=pltpu.CompilerParams(
-            collective_id=0, has_side_effects=True, vmem_limit_bytes=56 * 2**20
+            collective_id=0, has_side_effects=True, vmem_limit_bytes=36 * 2**20
         ),
         name="evolve",
-    )(start, aux, top, evaluate, back, trace, gather)
-    return pl.pallas_call(
-        functools.partial(unpack, capacity),
-        grid=(devices // share,),
-        out_shape=jax.ShapeDtypeStruct((MODES, MODES, MODES, devices * capacity), F32),
-        in_specs=[pl.BlockSpec((share, height, LANES), lambda t: (t, 0, 0))],
-        out_specs=pl.BlockSpec((MODES, MODES, MODES, LANES), lambda t: (0, 0, 0, t)),
-        scratch_shapes=[pltpu.VMEM((share * height, LANES), F32)],
-        compiler_params=pltpu.CompilerParams(vmem_limit_bytes=32 * 2**20),
-        name="unpack",
-    )(blocks)
+    )(aux, top, start, evaluate, back, trace, gather)
 
 
 def solution(mesh):

time: 124 us -> 121 us (0.976)
  Pallas kernels: 115 us -> 110 us
  local copies, waits for them, and re-layouts: 8.67 us -> 10.3 us
    pallas_call x1 -> x0, Pallas kernels: 6.67 us -> none  [on_device(): pl.pallas_call(functools.partial(unpack, capacity), grid=(devices // shar...]
    pallas_call x1, Pallas kernels: 105 us -> 106 us  [on_device(): pl.pallas_call(functools.partial(evolve, wide, narrow, capacity), out_sha...]
    unnamed x18 -> x21, local copies, waits for them, and re-layouts: 8.67 us -> 10.3 us
where the time goes in v1:
time: 121 us; the launch traced here: 120 us
  Pallas kernels  110 us (91%)
  local copies, waits for them, and re-layouts  10.3 us (9%)
    pallas_call x1, Pallas kernels, on_device(): pl.pallas_call(functools.partial(evolve, wide, narrow, capacity), out_sha...  106 us
    unnamed x21, local copies, waits for them, and re-layouts  10.3 us
    pallas_call x1, Pallas kernels, on_device(): pl.pallas_call(functools.partial(arrange, devices, capacity), out_shape=(...  3.8 us

profile of v1, /device:TPU:0, one launch (start us, length us, event | category | flops | bytes accessed | tf_op | source)
XLA Modules:
  0.0 120.4 jit_solution(7822785219235117408)
XLA Ops:
  0.0 0.0 copy-start
  0.0 1.4 %copy-done = f32[7,7,7,1024]{3,2,1,0:T(8,128)S(1)} copy-done((f32[7,7,7,1024]{3,2,1,0:T(8,128)S(1)}, f32[7,7,7,1024]{3,2,1,0:T(8,128)}, u32[]{:S(2)}) %copy-start) | copy-done | bytes 1404952
  1.4 0.0 copy-start.5
  1.4 0.9 copy-done.5
  2.3 0.0 copy-start.6
  2.3 0.8 copy-done.6
  3.1 0.0 copy-start.7
  3.1 0.7 copy-done.7
  3.8 0.0 copy-start.8
  3.8 0.7 copy-done.8
  4.5 0.0 copy-start.9
  4.5 0.7 copy-done.9
  5.2 0.0 copy-start.1
  5.2 3.8 %arrange.1 = (f32[352,1024]{1,0:T(8,128)S(1)}, s32[8,1024]{1,0:T(8,128)S(1)}) custom-call(f32[7,7,7,1024]{3,2,1,0:T(8,128)S(1)} %copy-done, s32[8,128]{1,0:T(8,128)S(1)} %bitcast.3, s32[8,128]{1,0:T(8,128)S(1)} %bitcast.4, s32[6,1024]{1,0:T(8,128)S(1)} %copy-done.6, s32[8,128]{1,0:T(8,128)S(1)} %bitcast.5, s32[352,128]{1,0:T(8,128)S(1)} %copy-done.5), custom_call_target="tpu_custom_call" | custom-call | tf_op jit(solution)/shard_map/arrange/pallas_call | solution.py:478
  9.0 0.0 copy-done.1
  9.0 0.0 copy-start.2
  9.0 1.2 %copy-done.2 = bf16[2,672,352]{2,1,0:T(8,128)(2,1)S(1)} copy-done((bf16[2,672,352]{2,1,0:T(8,128)(2,1)S(1)}, bf16[2,672,352]{2,1,0:T(8,128)(2,1)}, u32[]{:S(2)}) %copy-start.2) | copy-done | bytes 946200
  10.2 0.0 copy-start.3
  10.2 1.1 copy-done.3
  11.3 0.0 copy-start.4
  11.3 1.1 copy-done.4
  12.5 106.3 %evolve.1 = f32[7,7,7,2048]{3,2,1,0:T(8,128)S(1)} custom-call(s32[8,1024]{1,0:T(8,128)S(1)} %get-tuple-element.7.aux_ref, s32[352,128]{1,0:T(8,128)S(1)} %copy-done.5, f32[352,1024]{1,0:T(8,128)S(1)} %get-tuple-element.8.start_at, bf16[2,512,352]{2,1,0:T(8,128)(2,1)S(1)} %copy-done.3, bf16[2,352,512]{2,1,0:T(8,128)(2,1)S(1)} %copy-done.4, ...), custom_call_target="tpu_custom_call" | custom-call | tf_op jit(solution)/shard_map/evolve/pallas_call | solution.py:498
  118.7 1.7 %copy.16 = f32[7,7,7,2048]{3,2,1,0:T(8,128)} copy(f32[7,7,7,2048]{3,2,1,0:T(8,128)S(1)} %evolve.1) | data formatting | bytes 5619712
Async XLA Ops:
  0.0 1.4 %copy-start = (f32[7,7,7,1024]{3,2,1,0:T(8,128)S(1)}, f32[7,7,7,1024]{3,2,1,0:T(8,128)}, u32[]{:S(2)}) copy-start(f32[7,7,7,1024]{3,2,1,0:T(8,128)} %coef_ref.1) | copy-start | bytes 4214788
  1.4 0.9 copy-start.5
  2.3 0.8 copy-start.6
  3.1 0.7 copy-start.7
  3.8 0.7 copy-start.8
  4.5 0.7 copy-start.9
  5.2 3.8 %copy-start.1 = (bf16[2,352,1024]{2,1,0:T(8,128)(2,1)S(1)}, bf16[2,352,1024]{2,1,0:T(8,128)(2,1)}, u32[]{:S(2)}) copy-start(bf16[2,352,1024]{2,1,0:T(8,128)(2,1)} %constant.38.gather_at) | copy-start | bytes 4325380
  9.0 1.2 %copy-start.2 = (bf16[2,672,352]{2,1,0:T(8,128)(2,1)S(1)}, bf16[2,672,352]{2,1,0:T(8,128)(2,1)}, u32[]{:S(2)}) copy-start(bf16[2,672,352]{2,1,0:T(8,128)(2,1)} %constant.35.trace_at) | copy-start | bytes 2838532
  10.2 1.1 copy-start.3
  11.3 1.1 copy-start.4

commit v2 on v1

--- a/solution.py
+++ b/solution.py
@@ -60,6 +60,8 @@
         np.stack([(-1.0) ** (orders + 1), np.ones(MODES)]) * (orders * (orders + 1) / 2.0) * scales
     )
     eye = np.eye(MODES)
+    scaled = np.ones(ROWS)
+    scaled[: MODES**3] = np.kron(scales, np.kron(scales, scales))
 
     def kron(first, second, third):
         return np.kron(first, np.kron(second, third))
@@ -69,26 +71,39 @@
     evaluate[:, :modes] = kron(values, values, values)
     back = np.zeros((ROWS, QUAD**3))
     back[:modes] = kron(project, project, project)
+    back = back * scaled[:, None]
+    gather = np.zeros((ROWS, TRACE + ROWS))
     trace = np.zeros((TRACE, ROWS))
     plane = MODES**2
     for face in range(6):
         axis, side = divmod(face, 2)
         for kind, vector in enumerate((ends[side], end_slopes[side])):
             parts = [eye, eye, eye]
-            parts[axis] = vector[None, :]
+            parts[axis] = (vector / scales)[None, :]
             base = face * PAIR + kind * FACE
             trace[base : base + plane, :modes] = kron(*parts)
+            parts[axis] = (vector * scales / (1.0, 3.0)[kind])[:, None]
+            gather[:modes, base : base + plane] = kron(*parts)
     inner = kron(stiffness, eye, eye) + kron(eye, stiffness, eye) + kron(eye, eye, stiffness)
-    gather = np.zeros((ROWS, TRACE + ROWS))
-    gather[:, :TRACE] = trace.T
-    gather[:modes, TRACE : TRACE + modes] = -inner
-    return evaluate, back, trace, gather
-
-
-def host_halves(array):
+    diagonal = np.zeros(ROWS)
+    diagonal[:modes] = -np.diag(inner)
+    ratio = scaled[:modes, None] / scaled[None, :modes]
+    gather[:modes, TRACE : TRACE + modes] = (np.diag(np.diag(inner)) - inner) * ratio
+    rates = STEP_SIZE * np.stack([1.0 / scaled, diagonal / scaled])
+    rates = np.repeat(rates[:, :, None], LANES, axis=2).astype(np.float32)
+    return thrice(evaluate), thrice(back), twice(trace), twice(gather), jnp.asarray(rates)
+
+
+def thrice(array):
     high = array.astype(jnp.bfloat16)
     low = (array - high.astype(np.float64)).astype(jnp.bfloat16)
-    return jnp.stack([jnp.asarray(high), jnp.asarray(low)])
+    return jnp.asarray(np.concatenate([high, high, low], axis=1))
+
+
+def twice(array):
+    high = array.astype(jnp.bfloat16)
+    assert np.abs(high.astype(np.float64) - array).max() < 1e-9
+    return jnp.asarray(np.concatenate([high, high], axis=1))
 
 
 def highest_modes():
@@ -104,11 +119,9 @@
     return high, (array - high.astype(F32)).astype(BF16)
 
 
-def product(table_ref, high, low):
-    def dot(left, right):
-        return jnp.dot(left, right, preferred_element_type=F32)
-
-    return dot(table_ref[0], high) + (dot(table_ref[0], low) + dot(table_ref[1], high))
+def product(table_ref, *pieces):
+    stacked = jnp.concatenate(pieces, axis=0)
+    return jnp.dot(table_ref[...], stacked, preferred_element_type=F32)
 
 
 def take(table, index):
@@ -187,9 +200,9 @@
 
 
 def evolve(
-    wide, narrow, capacity, aux_ref, top_ref, start_at, eval_at, back_at, trace_at, gather_at,
+    wide, narrow, capacity, aux_ref, top_ref, rates_ref, start_at, eval_at, back_at, trace_at, gather_at,
     moved_ref,
-    start_ref, eval_ref, back_ref, trace_ref, gather_ref, table_sem, recv_ref, flat_ref, state_ref, face_refs, up_ref, down_ref, high_ref, low_ref, pair_ref, send_ref,
+    start_ref, eval_ref, back_ref, trace_ref, gather_ref, table_sem, recv_ref, flat_ref, state_ref, face_refs, up_ref, down_ref, both_ref, pair_ref, send_ref,
     z_out, z_in, halo_send, halo_recv, send_sem, recv_sem,
 ):
     devices = wide * narrow
@@ -215,6 +228,7 @@
 
     lax.fori_loop(1, devices, greet, 0)
     top = top_ref[:, :1]
+    half = TRACE + ROWS
     iota = lax.broadcasted_iota
     lane = iota(jnp.int32, (PAIR, LANES), 1)
     flip = jnp.where(iota(jnp.int32, (PAIR, LANES), 0) < FACE, -1.0, 1.0)
@@ -222,12 +236,15 @@
     def local_part(source_ref):
         def body(c, carry):
             at = pl.ds(pl.multiple_of(c * WORK, WORK), WORK)
-            values = product(eval_ref, *split(source_ref[:, at]))
+            high, low = split(source_ref[:, at])
+            values = product(eval_ref, high, low, high)
             values = values + values * values * values * (1.0 / 3.0)
-            field = jnp.where(top <= aux_ref[0:1, at], product(back_ref, *split(values)), 0.0)
+            high, low = split(values)
+            field = product(back_ref, high, low, high)
+            field = jnp.where(top <= aux_ref[0:1, at], field, 0.0)
             high, low = split(field)
-            high_ref[TRACE:, at] = high
-            low_ref[TRACE:, at] = low
+            both_ref[TRACE:half, at] = high
+            both_ref[half + TRACE :, at] = low
             traces = product(trace_ref, high, low)
             down_ref[:, at] = traces[:PAIR]
             up_ref[:, pl.ds(pl.multiple_of(c * WORK + LANES, LANES), WORK)] = traces[
@@ -335,16 +352,18 @@
             sums = own[FACE:] + ghost[FACE:]
             base = face * PAIR
             both = jnp.concatenate(
-                [(0.5 * sign) * sums - sigma * jump, (0.5 * sign) * jump], axis=0
+                [(0.5 * sign) * sums - sigma * jump, (1.5 * sign) * jump], axis=0
             )
             high, low = split(both)
-            high_ref[base : base + PAIR, at] = high
-            low_ref[base : base + PAIR, at] = low
+            both_ref[base : base + PAIR, at] = high
+            both_ref[half + base : half + base + PAIR, at] = low
 
     def residual(c):
         at = pl.ds(pl.multiple_of(c * WORK, WORK), WORK)
-        rate = product(gather_ref, high_ref[:, at], low_ref[:, at])
-        return at, jnp.where(top <= aux_ref[0:1, at], rate, 0.0) * STEP_SIZE
+        change = jnp.dot(gather_ref[...], both_ref[:, at], preferred_element_type=F32)
+        field = both_ref[TRACE:half, at].astype(F32) + both_ref[half + TRACE :, at].astype(F32)
+        change = change * rates_ref[0, :, :1] + field * rates_ref[1, :, :1]
+        return at, jnp.where(top <= aux_ref[0:1, at], change, 0.0)
 
     def section(turn, source_ref, before_send, store):
         local_part(source_ref)
@@ -471,7 +490,7 @@
     share = LANES // capacity
     modes = MODES**3
     height = -(-(-(-modes // share)) // 8) * 8
-    evaluate, back, trace, gather = (host_halves(array) for array in operators())
+    evaluate, back, trace, gather, rates = operators()
     top = highest_modes()
     vmem = pl.BlockSpec(memory_space=pltpu.VMEM)
     square = (SIDE, LANES)
@@ -498,7 +517,7 @@
     return pl.pallas_call(
         functools.partial(evolve, wide, narrow, capacity),
         out_shape=jax.ShapeDtypeStruct((MODES, MODES, MODES, devices * capacity), F32),
-        in_specs=[vmem] * 2 + [anywhere] * 5,
+        in_specs=[vmem] * 3 + [anywhere] * 5,
         out_specs=vmem,
         scratch_shapes=[
             pltpu.VMEM((ROWS, count), F32),
@@ -513,8 +532,7 @@
             pltpu.VMEM((4, PAIR, count), F32),
             pltpu.VMEM((PAIR, count + LANES), F32),
             pltpu.VMEM((PAIR, count + LANES), F32),
-            pltpu.VMEM((TRACE + ROWS, count), BF16),
-            pltpu.VMEM((TRACE + ROWS, count), BF16),
+            pltpu.VMEM((2 * (TRACE + ROWS), count), BF16),
             pltpu.VMEM((2 * ROWS, count), BF16),
             pltpu.VMEM((devices, height, LANES), F32),
             pltpu.VMEM((2, 4, PAIR, LANES), F32),
@@ -528,7 +546,7 @@
             collective_id=0, has_side_effects=True, vmem_limit_bytes=36 * 2**20
         ),
         name="evolve",
-    )(aux, top, start, evaluate, back, trace, gather)
+    )(aux, top, rates, start, evaluate, back, trace, gather)
 
 
 def solution(mesh):

time: 121 us -> 116 us (0.959)
  Pallas kernels: 110 us -> 105 us
    pallas_call x1, Pallas kernels: 106 us -> 101 us  [on_device(): pl.pallas_call(functools.partial(evolve, wide, narrow, capacity), out_sha...]
    unnamed x21 -> x23, local copies, waits for them, and re-layouts: 10.3 us -> 10.6 us
where the time goes in v2:
time: 116 us
  Pallas kernels  105 us (91%)
  local copies, waits for them, and re-layouts  10.6 us (9%)
    pallas_call x1, Pallas kernels, on_device(): pl.pallas_call(functools.partial(evolve, wide, narrow, capacity), out_sha...  101 us
    unnamed x23, local copies, waits for them, and re-layouts  10.6 us
    pallas_call x1, Pallas kernels, on_device(): pl.pallas_call(functools.partial(arrange, devices, capacity), out_shape=(...  3.8 us

profile of v2, /device:TPU:0, one launch (start us, length us, event | category | flops | bytes accessed | tf_op | source)
XLA Modules:
  0.0 115.8 jit_solution(2622912961712082953)
XLA Ops:
  0.0 0.0 copy-start
  0.0 1.4 %copy-done = f32[7,7,7,1024]{3,2,1,0:T(8,128)S(1)} copy-done((f32[7,7,7,1024]{3,2,1,0:T(8,128)S(1)}, f32[7,7,7,1024]{3,2,1,0:T(8,128)}, u32[]{:S(2)}) %copy-start) | copy-done | bytes 1404952
  1.4 0.0 copy-start.5
  1.4 0.9 copy-done.5
  2.3 0.0 copy-start.7
  2.3 0.8 copy-done.7
  3.1 0.0 copy-start.8
  3.1 0.7 copy-done.8
  3.8 0.0 copy-start.9
  3.8 0.7 copy-done.9
  4.5 0.0 copy-start.10
  4.5 0.7 copy-done.10
  5.2 0.0 copy-start.1
  5.2 0.0 copy-start.6
  5.2 3.8 %arrange.1 = (f32[352,1024]{1,0:T(8,128)S(1)}, s32[8,1024]{1,0:T(8,128)S(1)}) custom-call(f32[7,7,7,1024]{3,2,1,0:T(8,128)S(1)} %copy-done, s32[8,128]{1,0:T(8,128)S(1)} %bitcast.3, s32[8,128]{1,0:T(8,128)S(1)} %bitcast.4, s32[6,1024]{1,0:T(8,128)S(1)} %copy-done.7, s32[8,128]{1,0:T(8,128)S(1)} %bitcast.5, s32[352,128]{1,0:T(8,128)S(1)} %copy-done.5), custom_call_target="tpu_custom_call" | custom-call | tf_op jit(solution)/shard_map/arrange/pallas_call | solution.py:497
  9.0 0.0 copy-done.1
  9.0 0.0 copy-done.6
  9.0 0.0 copy-start.2
  9.0 1.3 %copy-done.2 = bf16[512,1056]{1,0:T(8,128)(2,1)S(1)} copy-done((bf16[512,1056]{1,0:T(8,128)(2,1)S(1)}, bf16[512,1056]{1,0:T(8,128)(2,1)}, u32[]{:S(2)}) %copy-start.2) | copy-done | bytes 1081368
  10.3 0.0 copy-start.3
  10.3 1.2 %copy-done.3 = bf16[352,1536]{1,0:T(8,128)(2,1)S(1)} copy-done((bf16[352,1536]{1,0:T(8,128)(2,1)S(1)}, bf16[352,1536]{1,0:T(8,128)(2,1)}, u32[]{:S(2)}) %copy-start.3) | copy-done | bytes 1081368
  11.5 0.0 copy-start.4
  11.5 1.2 %copy-done.4 = bf16[672,704]{1,0:T(8,128)(2,1)S(1)} copy-done((bf16[672,704]{1,0:T(8,128)(2,1)S(1)}, bf16[672,704]{1,0:T(8,128)(2,1)}, u32[]{:S(2)}) %copy-start.4) | copy-done | bytes 946200
  12.7 101.4 %evolve.1 = f32[7,7,7,2048]{3,2,1,0:T(8,128)S(1)} custom-call(s32[8,1024]{1,0:T(8,128)S(1)} %get-tuple-element.7.aux_ref, s32[352,128]{1,0:T(8,128)S(1)} %copy-done.5, f32[2,352,128]{2,1,0:T(8,128)S(1)} %copy-done.6, f32[352,1024]{1,0:T(8,128)S(1)} %get-tuple-element.8.start_at, bf16[512,1056]{1,0:T(8,128)(2,1)S(1)} %copy-done.2, ...), custom_call_target="tpu_custom_call" | custom-call | tf_op jit(solution)/shard_map/evolve/pallas_call | solution.py:517
  114.1 1.7 %copy.13 = f32[7,7,7,2048]{3,2,1,0:T(8,128)} copy(f32[7,7,7,2048]{3,2,1,0:T(8,128)S(1)} %evolve.1) | data formatting | bytes 5619712
Async XLA Ops:
  0.0 1.4 %copy-start = (f32[7,7,7,1024]{3,2,1,0:T(8,128)S(1)}, f32[7,7,7,1024]{3,2,1,0:T(8,128)}, u32[]{:S(2)}) copy-start(f32[7,7,7,1024]{3,2,1,0:T(8,128)} %coef_ref.1) | copy-start | bytes 4214788
  1.4 0.9 copy-start.5
  2.3 0.8 copy-start.7
  3.1 0.7 copy-start.8
  3.8 0.7 copy-start.9
  4.5 0.7 copy-start.10
  5.2 3.8 %copy-start.1 = (bf16[352,2048]{1,0:T(8,128)(2,1)S(1)}, bf16[352,2048]{1,0:T(8,128)(2,1)}, u32[]{:S(2)}) copy-start(bf16[352,2048]{1,0:T(8,128)(2,1)} %constant.15.clone.gather_at) | copy-start | bytes 4325380
  5.2 3.8 %copy-start.6 = (f32[2,352,128]{2,1,0:T(8,128)S(1)}, f32[2,352,128]{2,1,0:T(8,128)}, u32[]{:S(2)}) copy-start(f32[2,352,128]{2,1,0:T(8,128)} %constant.16.clone.rates_ref) | copy-start | bytes 1081348
  9.0 1.3 %copy-start.2 = (bf16[512,1056]{1,0:T(8,128)(2,1)S(1)}, bf16[512,1056]{1,0:T(8,128)(2,1)}, u32[]{:S(2)}) copy-start(bf16[512,1056]{1,0:T(8,128)(2,1)} %constant.12.clone.eval_at) | copy-start | bytes 3244036
  10.3 1.2 %copy-start.3 = (bf16[352,1536]{1,0:T(8,128)(2,1)S(1)}, bf16[352,1536]{1,0:T(8,128)(2,1)}, u32[]{:S(2)}) copy-start(bf16[352,1536]{1,0:T(8,128)(2,1)} %constant.13.clone.back_at) | copy-start | bytes 3244036
  11.5 1.2 %copy-start.4 = (bf16[672,704]{1,0:T(8,128)(2,1)S(1)}, bf16[672,704]{1,0:T(8,128)(2,1)}, u32[]{:S(2)}) copy-start(bf16[672,704]{1,0:T(8,128)(2,1)} %constant.14.clone.trace_at) | copy-start | bytes 2838532

commit v3 on v2

--- a/solution.py
+++ b/solution.py
@@ -17,7 +17,7 @@
 FACE = 56
 PAIR = 2 * FACE
 TRACE = 6 * PAIR
-WORK = 256
+WORK = 512
 STEP_SIZE = 0.0003
 MESH = pl.DeviceIdType.MESH
 F32 = jnp.float32

time: 116 us -> 109 us (0.940)
  Pallas kernels: 105 us -> 97.4 us
    pallas_call x1, Pallas kernels: 101 us -> 94 us  [on_device(): pl.pallas_call(functools.partial(evolve, wide, narrow, capacity), out_sha...]
where the time goes in v3:
time: 109 us; the launch traced here: 108 us
  Pallas kernels  97.4 us (89%)
  local copies, waits for them, and re-layouts  10.6 us (10%)
    pallas_call x1, Pallas kernels, on_device(): pl.pallas_call(functools.partial(evolve, wide, narrow, capacity), out_sha...  94 us
    unnamed x23, local copies, waits for them, and re-layouts  10.6 us
    pallas_call x1, Pallas kernels, on_device(): pl.pallas_call(functools.partial(arrange, devices, capacity), out_shape=(...  3.47 us

profile of v3, /device:TPU:0, one launch (start us, length us, event | category | flops | bytes accessed | tf_op | source)
XLA Modules:
  0.0 108.1 jit_solution(7781739636704895447)
XLA Ops:
  0.0 0.0 copy-start
  0.0 1.4 %copy-done = f32[7,7,7,1024]{3,2,1,0:T(8,128)S(1)} copy-done((f32[7,7,7,1024]{3,2,1,0:T(8,128)S(1)}, f32[7,7,7,1024]{3,2,1,0:T(8,128)}, u32[]{:S(2)}) %copy-start) | copy-done | bytes 1404952
  1.4 0.0 copy-start.5
  1.4 0.9 copy-done.5
  2.3 0.0 copy-start.7
  2.3 0.8 copy-done.7
  3.1 0.0 copy-start.8
  3.1 0.7 copy-done.8
  3.8 0.0 copy-start.9
  3.8 0.7 copy-done.9
  4.5 0.0 copy-start.10
  4.5 0.7 copy-done.10
  5.2 0.0 copy-start.1
  5.2 0.0 copy-start.6
  5.2 3.5 %arrange.1 = (f32[352,1024]{1,0:T(8,128)S(1)}, s32[8,1024]{1,0:T(8,128)S(1)}) custom-call(f32[7,7,7,1024]{3,2,1,0:T(8,128)S(1)} %copy-done, s32[8,128]{1,0:T(8,128)S(1)} %bitcast.3, s32[8,128]{1,0:T(8,128)S(1)} %bitcast.4, s32[6,1024]{1,0:T(8,128)S(1)} %copy-done.7, s32[8,128]{1,0:T(8,128)S(1)} %bitcast.5, s32[352,128]{1,0:T(8,128)S(1)} %copy-done.5), custom_call_target="tpu_custom_call" | custom-call | tf_op jit(solution)/shard_map/arrange/pallas_call | solution.py:497
  8.6 0.0 copy-done.1
  8.7 0.0 copy-done.6
  8.7 0.0 copy-start.2
  8.7 1.3 %copy-done.2 = bf16[512,1056]{1,0:T(8,128)(2,1)S(1)} copy-done((bf16[512,1056]{1,0:T(8,128)(2,1)S(1)}, bf16[512,1056]{1,0:T(8,128)(2,1)}, u32[]{:S(2)}) %copy-start.2) | copy-done | bytes 1081368
  9.9 0.0 copy-start.3
  9.9 1.2 %copy-done.3 = bf16[352,1536]{1,0:T(8,128)(2,1)S(1)} copy-done((bf16[352,1536]{1,0:T(8,128)(2,1)S(1)}, bf16[352,1536]{1,0:T(8,128)(2,1)}, u32[]{:S(2)}) %copy-start.3) | copy-done | bytes 1081368
  11.2 0.0 copy-start.4
  11.2 1.2 %copy-done.4 = bf16[672,704]{1,0:T(8,128)(2,1)S(1)} copy-done((bf16[672,704]{1,0:T(8,128)(2,1)S(1)}, bf16[672,704]{1,0:T(8,128)(2,1)}, u32[]{:S(2)}) %copy-start.4) | copy-done | bytes 946200
  12.4 94.0 %evolve.1 = f32[7,7,7,2048]{3,2,1,0:T(8,128)S(1)} custom-call(s32[8,1024]{1,0:T(8,128)S(1)} %get-tuple-element.7.aux_ref, s32[352,128]{1,0:T(8,128)S(1)} %copy-done.5, f32[2,352,128]{2,1,0:T(8,128)S(1)} %copy-done.6, f32[352,1024]{1,0:T(8,128)S(1)} %get-tuple-element.8.start_at, bf16[512,1056]{1,0:T(8,128)(2,1)S(1)} %copy-done.2, ...), custom_call_target="tpu_custom_call" | custom-call | tf_op jit(solution)/shard_map/evolve/pallas_call | solution.py:517
  106.4 1.7 %copy.13 = f32[7,7,7,2048]{3,2,1,0:T(8,128)} copy(f32[7,7,7,2048]{3,2,1,0:T(8,128)S(1)} %evolve.1) | data formatting | bytes 5619712
Async XLA Ops:
  0.0 1.4 %copy-start = (f32[7,7,7,1024]{3,2,1,0:T(8,128)S(1)}, f32[7,7,7,1024]{3,2,1,0:T(8,128)}, u32[]{:S(2)}) copy-start(f32[7,7,7,1024]{3,2,1,0:T(8,128)} %coef_ref.1) | copy-start | bytes 4214788
  1.4 0.9 copy-start.5
  2.3 0.8 copy-start.7
  3.1 0.7 copy-start.8
  3.8 0.7 copy-start.9
  4.5 0.7 copy-start.10
  5.2 3.5 %copy-start.1 = (bf16[352,2048]{1,0:T(8,128)(2,1)S(1)}, bf16[352,2048]{1,0:T(8,128)(2,1)}, u32[]{:S(2)}) copy-start(bf16[352,2048]{1,0:T(8,128)(2,1)} %constant.15.clone.gather_at) | copy-start | bytes 4325380
  5.2 3.5 %copy-start.6 = (f32[2,352,128]{2,1,0:T(8,128)S(1)}, f32[2,352,128]{2,1,0:T(8,128)}, u32[]{:S(2)}) copy-start(f32[2,352,128]{2,1,0:T(8,128)} %constant.16.clone.rates_ref) | copy-start | bytes 1081348
  8.7 1.3 %copy-start.2 = (bf16[512,1056]{1,0:T(8,128)(2,1)S(1)}, bf16[512,1056]{1,0:T(8,128)(2,1)}, u32[]{:S(2)}) copy-start(bf16[512,1056]{1,0:T(8,128)(2,1)} %constant.12.clone.eval_at) | copy-start | bytes 3244036
  9.9 1.2 %copy-start.3 = (bf16[352,1536]{1,0:T(8,128)(2,1)S(1)}, bf16[352,1536]{1,0:T(8,128)(2,1)}, u32[]{:S(2)}) copy-start(bf16[352,1536]{1,0:T(8,128)(2,1)} %constant.13.clone.back_at) | copy-start | bytes 3244036
  11.2 1.2 %copy-start.4 = (bf16[672,704]{1,0:T(8,128)(2,1)S(1)}, bf16[672,704]{1,0:T(8,128)(2,1)}, u32[]{:S(2)}) copy-start(bf16[672,704]{1,0:T(8,128)(2,1)} %constant.14.clone.trace_at) | copy-start | bytes 2838532
